TPU v7x, 32 devices: a whole 2x2x4 slice. The times are simulated.
32 devices in a mesh: gx: 16 (over z, y, core), gy: 2 (over x).
Axes of the slice: x: 2, y: 2, z: 4, core: 2. Of those that a mesh axis runs over, the one named last changes fastest.
Arguments:
- latents: int32 [768, 64, 32], P('gy', 'gx'), may hold values from 0 to 31
- actions: int32 [768, 64], P('gy', 'gx'), may hold values from 0 to 17
- segment_ids: int32 [768, 64], replicated, may hold values from 0 to 3, never falling along the last dimension, each value on 1 to 32 neighbouring positions
- cotangent: bfloat16 [768, 64, 512], P('gy', 'gx'), may hold values from -6 to 6
- stem_weight: bfloat16 [1024, 512], replicated, may hold values from -1 to 1
- action_table: bfloat16 [18, 512], replicated, may hold values from -1 to 1
- first_gain: float32 [512], replicated, may hold values from 0.5 to 1.5
- first_bias: float32 [512], replicated, may hold values from -1 to 1
- query_weight: bfloat16 [512, 512], P(None, 'gy'), may hold values from -0.25 to 0.25
- key_weight: bfloat16 [512, 512], P(None, 'gy'), may hold values from -0.25 to 0.25
- value_weight: bfloat16 [512, 512], P(None, 'gy'), may hold values from -0.25 to 0.25
- out_weight: bfloat16 [512, 512], P('gy'), may hold values from -1 to 1
- second_gain: float32 [512], replicated, may hold values from 0.5 to 1.5
- second_bias: float32 [512], replicated, may hold values from -1 to 1
- up_weight: bfloat16 [512, 2048], P(None, 'gy'), may hold values from -0.25 to 0.25
- up_bias: float32 [2048], P('gy'), may hold values from -1 to 1
- down_weight: bfloat16 [2048, 512], P('gy'), may hold values from -0.125 to 0.125
- down_bias: float32 [512], replicated, may hold values from -1 to 1
Outputs:
- output: bfloat16 [768, 64, 512], P('gy', 'gx')
- token_grad: bfloat16 [768, 64, 512], P('gy', 'gx')
- stem_grad: float32 [1024, 512], replicated
- action_grad: float32 [18, 512], replicated
- first_gain_grad: float32 [512], replicated
- first_bias_grad: float32 [512], replicated
- query_grad: float32 [512, 512], P(None, 'gy')
- key_grad: float32 [512, 512], P(None, 'gy')
- value_grad: float32 [512, 512], P(None, 'gy')
- out_grad: float32 [512, 512], P('gy')
- second_gain_grad: float32 [512], replicated
- second_bias_grad: float32 [512], replicated
- up_grad: float32 [512, 2048], P(None, 'gy')
- up_bias_grad: float32 [2048], P('gy')
- down_grad: float32 [2048, 512], P('gy')
- down_bias_grad: float32 [512], replicated
Inputs may be any that keep to these rules, and one draw needn't show every extreme that they name: `segment_ids`: along each sequence of 64 frames the segment id never falls; each segment holds 1 to 32 frames.
All inputs are finite; a program needn't handle non-finite values.
Results may differ from a plain program's by a relative error of at most 0.012.
Values may be sent and summed in bfloat16 or wider, within the bound.
A program may use at most 192 MiB of HBM per device.

v0:
```python
import jax
import jax.numpy as jnp
from jax import lax
from jax.sharding import PartitionSpec as P

HD = 64
EPSILON = 1e-05
FLOAT = jnp.float32
BFLOAT = jnp.bfloat16


def norm_rows(values, gain, bias):
    average = jnp.mean(values, axis=-1, keepdims=True)
    centred = values - average
    spread = jnp.mean(centred * centred, axis=-1, keepdims=True)
    return centred * lax.rsqrt(spread + EPSILON) * gain + bias


def inner(left, right):
    return lax.dot_general(left, right, (((0,), (0,)), ((), ())), preferred_element_type=FLOAT)


def outer(left, right):
    return lax.dot_general(left, right, (((1,), (1,)), ((), ())), preferred_element_type=FLOAT)


def product(left, right):
    return jnp.dot(left, right, preferred_element_type=FLOAT)


def split_heads(block):
    return block.reshape(block.shape[0], block.shape[1], -1, HD)


def block_probs(query_block, key_block, label_block):
    length = query_block.shape[1]
    scores = 0.125 * jnp.einsum(
        "sqhd,skhd->shqk",
        split_heads(query_block),
        split_heads(key_block),
        preferred_element_type=FLOAT,
    )
    place = jnp.arange(length)
    allowed = (label_block[:, :, None] == label_block[:, None, :]) & (
        place[:, None] >= place[None, :]
    )[None]
    return jax.nn.softmax(jnp.where(allowed[:, None], scores, -1e30), axis=-1)


def block_forward(pieces):
    query_block, key_block, value_block, label_block = pieces
    probs_low = block_probs(query_block, key_block, label_block).astype(BFLOAT)
    mixed = jnp.einsum(
        "shqk,skhd->sqhd", probs_low, split_heads(value_block), preferred_element_type=FLOAT
    )
    return mixed.reshape(query_block.shape[0], query_block.shape[1], -1).astype(BFLOAT)


def block_backward(pieces):
    query_block, key_block, value_block, label_block, grad_block = pieces
    probs = block_probs(query_block, key_block, label_block)
    grad_heads = split_heads(grad_block)
    grad_probs = jnp.einsum(
        "sqhd,skhd->shqk", grad_heads, split_heads(value_block), preferred_element_type=FLOAT
    )
    grad_probs = lax.optimization_barrier(grad_probs.astype(BFLOAT)).astype(FLOAT)
    centre = jnp.sum(probs * grad_probs, axis=-1, keepdims=True)
    grad_scores = (probs * (grad_probs - centre)).astype(BFLOAT)
    grad_query = 0.125 * jnp.einsum(
        "shqk,skhd->sqhd", grad_scores, split_heads(key_block), preferred_element_type=FLOAT
    )
    grad_key = 0.125 * jnp.einsum(
        "shqk,sqhd->skhd", grad_scores, split_heads(query_block), preferred_element_type=FLOAT
    )
    grad_value = jnp.einsum(
        "shqk,sqhd->skhd", probs.astype(BFLOAT), grad_heads, preferred_element_type=FLOAT
    )
    shape = (query_block.shape[0], query_block.shape[1], -1)
    return tuple(
        (item.reshape(shape).astype(BFLOAT) for item in (grad_query, grad_key, grad_value))
    )


def layer_pass(seq_tokens, seq_cot, seg_rows, weights):
    (
        first_gain,
        first_bias,
        query_weight,
        key_weight,
        value_weight,
        out_weight,
        second_gain,
        second_bias,
        up_weight,
        up_bias,
        down_weight,
        down_bias,
    ) = weights
    seqs, length, width = seq_tokens.shape
    rows = seqs * length
    block = min(512, rows)
    blocks = rows // block
    within = block // length
    scale = 0.5
    inputs = seq_tokens.reshape(rows, width).astype(FLOAT)
    normed_one = norm_rows(inputs, first_gain, first_bias).astype(BFLOAT)
    query = product(normed_one, query_weight).astype(BFLOAT)
    key_rows = product(normed_one, key_weight).astype(BFLOAT)
    value_rows = product(normed_one, value_weight).astype(BFLOAT)
    labels = seg_rows.reshape(blocks, within, length)

    def split_rows(array):
        return array.reshape(blocks, within, length, -1)

    mixed = lax.map(
        block_forward, (split_rows(query), split_rows(key_rows), split_rows(value_rows), labels)
    )
    mixed = mixed.reshape(rows, -1)
    branch = product(mixed, out_weight)
    branch = lax.psum(branch, "gy")
    resid = inputs + branch
    normed_two = norm_rows(resid, second_gain, second_bias).astype(BFLOAT)
    pre_act = product(normed_two, up_weight) + up_bias
    hidden = jax.nn.gelu(pre_act).astype(BFLOAT)
    out_part = scale * (resid + down_bias) + product(hidden, down_weight)
    cot_rows = seq_cot.reshape(rows, width)
    cot_float = cot_rows.astype(FLOAT)
    down_bias_part = jnp.sum(cot_float, axis=0)
    down_part = inner(hidden, cot_rows)
    d_hidden = outer(cot_rows, down_weight)
    act_input = product(normed_two, up_weight) + up_bias
    _, gelu_pull = jax.vjp(jax.nn.gelu, act_input)
    d_pre = gelu_pull(d_hidden)[0].astype(BFLOAT)
    up_bias_part = jnp.sum(d_pre.astype(FLOAT), axis=0)
    up_part = inner(normed_two, d_pre)
    d_normed_two = outer(d_pre, up_weight)
    d_normed_two = lax.psum(d_normed_two, "gy")
    _, second_pull = jax.vjp(norm_rows, resid, second_gain, second_bias)
    d_resid_norm, second_gain_part, second_bias_part = second_pull(d_normed_two)
    d_resid = cot_float + d_resid_norm
    d_branch = d_resid.astype(BFLOAT)
    out_part_grad = inner(mixed, d_branch)
    d_mixed = outer(d_branch, out_weight).astype(BFLOAT)
    d_query, d_key, d_value = lax.map(
        block_backward,
        (
            split_rows(query),
            split_rows(key_rows),
            split_rows(value_rows),
            labels,
            split_rows(d_mixed),
        ),
    )
    d_query = d_query.reshape(rows, -1)
    d_key = d_key.reshape(rows, -1)
    d_value = d_value.reshape(rows, -1)
    query_part = inner(normed_one, d_query)
    key_part = inner(normed_one, d_key)
    value_part = inner(normed_one, d_value)
    d_normed_one = (
        outer(d_query, query_weight) + outer(d_key, key_weight) + outer(d_value, value_weight)
    )
    _, first_pull = jax.vjp(norm_rows, inputs, first_gain, first_bias)
    d_input_norm, first_gain_part, first_bias_part = first_pull(d_normed_one)
    d_tokens_part = scale * d_resid + d_input_norm
    parts = (
        first_gain_part,
        first_bias_part,
        query_part,
        key_part,
        value_part,
        out_part_grad,
        second_gain_part,
        second_bias_part,
        up_part,
        up_bias_part,
        down_part,
        down_bias_part,
    )
    return (
        out_part.reshape(seqs, length, width),
        d_tokens_part.reshape(seqs, length, width),
        parts,
    )


def per_device(
    latents,
    actions,
    segment_ids,
    cotangent,
    stem_weight,
    action_table,
    first_gain,
    first_bias,
    query_weight,
    key_weight,
    value_weight,
    out_weight,
    second_gain,
    second_bias,
    up_weight,
    up_bias,
    down_weight,
    down_bias,
):
    half_seqs, local_len, groups = latents.shape
    frames = half_seqs * local_len
    classes = stem_weight.shape[0] // groups
    latent_hot = (latents[..., None] == jnp.arange(classes, dtype=jnp.int32)).reshape(
        frames, groups * classes
    )
    latent_hot = latent_hot.astype(BFLOAT)
    action_hot = (
        actions.reshape(frames, 1) == jnp.arange(action_table.shape[0], dtype=jnp.int32)[None, :]
    )
    action_hot = action_hot.astype(BFLOAT)
    stem = product(latent_hot, stem_weight) + product(action_hot, action_table)
    tokens = stem.astype(BFLOAT).reshape(half_seqs, local_len, -1)
    token_all, cot_all = (
        lax.all_gather(tokens, "gy", axis=0, tiled=True),
        lax.all_gather(cotangent, "gy", axis=0, tiled=True),
    )
    seq_tokens, seq_cot = (
        lax.all_to_all(token_all, "gx", split_axis=0, concat_axis=1, tiled=True),
        lax.all_to_all(cot_all, "gx", split_axis=0, concat_axis=1, tiled=True),
    )
    seqs = seq_tokens.shape[0]
    first_seq = lax.axis_index("gx") * seqs
    weights = (
        first_gain,
        first_bias,
        query_weight,
        key_weight,
        value_weight,
        out_weight,
        second_gain,
        second_bias,
        up_weight,
        up_bias,
        down_weight,
        down_bias,
    )
    seg_rows = lax.dynamic_slice_in_dim(segment_ids, first_seq, seqs, 0)
    out_seq, grad_seq, parts = layer_pass(seq_tokens, seq_cot, seg_rows, weights)
    out_moved, grad_moved = (
        lax.all_to_all(out_seq, "gx", split_axis=1, concat_axis=0, tiled=True),
        lax.all_to_all(grad_seq, "gx", split_axis=1, concat_axis=0, tiled=True),
    )
    out_frames, grad_frames = (
        lax.psum_scatter(out_moved, "gy", scatter_dimension=0, tiled=True),
        lax.psum_scatter(grad_moved, "gy", scatter_dimension=0, tiled=True),
    )
    output = out_frames.astype(BFLOAT)
    token_grad = grad_frames.astype(BFLOAT)
    width = stem_weight.shape[1]
    grad_flat = token_grad.reshape(frames, width)
    stem_part = inner(latent_hot, grad_flat)
    action_part = inner(action_hot, grad_flat)
    (
        first_gain_part,
        first_bias_part,
        query_part,
        key_part,
        value_part,
        out_part_grad,
        second_gain_part,
        second_bias_part,
        up_part,
        up_bias_part,
        down_part,
        down_bias_part,
    ) = parts
    stem_grad, action_grad, first_gain_grad, first_bias_grad = lax.psum(
        (stem_part, action_part, first_gain_part, first_bias_part), ("gx", "gy")
    )
    (
        query_grad,
        key_grad,
        value_grad,
        out_grad,
        second_gain_grad,
        second_bias_grad,
        up_grad,
        up_bias_grad,
        down_grad,
        down_bias_grad,
    ) = lax.psum(
        (
            query_part,
            key_part,
            value_part,
            out_part_grad,
            second_gain_part,
            second_bias_part,
            up_part,
            up_bias_part,
            down_part,
            down_bias_part,
        ),
        "gx",
    )
    return (
        output,
        token_grad,
        stem_grad,
        action_grad,
        first_gain_grad,
        first_bias_grad,
        query_grad,
        key_grad,
        value_grad,
        out_grad,
        second_gain_grad,
        second_bias_grad,
        up_grad,
        up_bias_grad,
        down_grad,
        down_bias_grad,
    )


def solution(mesh):
    return jax.shard_map(
        per_device,
        mesh=mesh,
        in_specs=(
            P("gy", "gx", None),
            P("gy", "gx"),
            P(),
            P("gy", "gx", None),
            P(),
            P(),
            P(),
            P(),
            P(None, "gy"),
            P(None, "gy"),
            P(None, "gy"),
            P("gy", None),
            P(),
            P(),
            P(None, "gy"),
            P("gy"),
            P("gy", None),
            P(),
        ),
        out_specs=(
            P("gy", "gx", None),
            P("gy", "gx", None),
            P(),
            P(),
            P(),
            P(),
            P(None, "gy"),
            P(None, "gy"),
            P(None, "gy"),
            P("gy", None),
            P(),
            P(),
            P(None, "gy"),
            P("gy"),
            P("gy", None),
            P(),
        ),
        check_vma=False,
    )
```

profile of v0, /device:TPU:0, one launch (start us, length us, event | category | flops | bytes accessed | tf_op | source)
XLA Modules:
  0.0 1381.9 jit_solution(16798744642058293899)
XLA Ops:
  8.6 9.8 eq.86
  18.4 19.9 %eq.87 = s32[1536,1024]{1,0:T(8,128)} reshape(s32[384,4,32,32]{3,2,1,0:T(8,128)} %eq.86) | data formatting | bytes 12582912 | tf_op jit(solution)/shard_map/eq | solution.py:210
  38.7 4.8 fusion.28
  46.1 47.8 %all-gather.3.cloned.1.call-done = bf16[768,4,512]{2,1,0:T(4,128)(2,1)} async-done(((bf16[384,4,512]{2,1,0:T(4,128)(2,1)}), bf16[768,4,512]{2,1,0:T(4,128)(2,1)}) %all-gather.3.cloned.1.call-update) | async-done | bytes 3145744 | tf_op jit(solution)/shard_map/all_gather | solution.py:221
  93.9 5.7 all-to-all-start
  101.8 57.1 %all-to-all-done = bf16[768,4,512]{2,1,0:T(4,128)(2,1)} async-done(((bf16[768,4,512]{2,1,0:T(4,128)(2,1)}), bf16[768,4,512]{2,1,0:T(4,128)(2,1)}, u32[]{:S(2)}, u32[]{:S(2)}) %all-to-all-start) | async-done | bytes 3145760 | tf_op jit(solution)/shard_map/all_to_all | solution.py:225
  158.9 3.2 fusion.38
  162.2 4.4 multiply_reduce_fusion.5
  166.9 6.3 copy_bitcast_fusion
  174.3 7.6 reshape.397
  182.0 3.8 add_convert_fusion.2
  185.8 2.1 convolution_convert_fusion.6
  187.9 2.1 convolution_convert_fusion.5
  190.0 2.1 convolution_convert_fusion.4
  193.5 43.5 %while.24 = (s32[]{:T(128)}, bf16[6,8,64,256]{3,2,1,0:T(8,128)(2,1)}, bf16[6,8,64,256]{3,2,1,0:T(8,128)(2,1)}, s32[6,8,64]{2,1,0:T(8,128)S(1)}, bf16[6,8,64,256]...) while((s32[]{:T(128)}, bf16[6,8,64,256]{3,2,1,0:T(8,128)(2,1)}, ...), condition=%wide.region_5.6_spmd, body=%wide.region_2.5_spmd.sunk | while | flops 34674816 | bytes 9009781 | solution.py:115
  237.0 5.0 fusion.46
  242.1 85.4 %all_to_all.60 = bf16[768,4,512]{2,1,0:T(4,128)(2,1)S(1)} all-to-all(bf16[768,4,512]{2,1,0:T(4,128)(2,1)} %all-gather.5.cloned.1.call-done), channel_id=1, replica_groups=mesh['gx'=16,'gy'=2] {'gx'}, dimensions={0} | all-to-all | bytes 6291456 | tf_op jit(solution)/shard_map/all_to_all | solution.py:226
  329.1 3.4 copy.146
  332.5 5.7 reshape.390
  338.2 67.0 %all-reduce.12.cloned.1.call-done = f32[3072,512]{1,0:T(8,128)} async-done(((f32[3072,512]{1,0:T(8,128)}), f32[3072,512]{1,0:T(8,128)}) %all-reduce.12.cloned.1.call-update) | async-done | bytes 6291472 | tf_op jit(solution)/shard_map/psum | solution.py:120
  405.2 5.3 fusion.43
  410.5 2.1 multiply_reduce_fusion.4
  412.7 9.9 multiply_convert_fusion
  422.7 13.3 convert_reduce_fusion
  436.0 2.6 copy-done.57
  438.6 5.8 fusion.47
  445.0 9.6 multiply_add_fusion
  454.7 6.4 copy.108
  461.0 6.1 all-to-all-start.1
  467.1 130.6 %all-reduce.14.cloned.1.call-done = f32[3072,512]{1,0:T(8,128)} async-done(((f32[3072,512]{1,0:T(8,128)}), f32[3072,512]{1,0:T(8,128)}) %all-reduce.14.cloned.1.call-update) | async-done | bytes 6291472 | tf_op jit(solution)/shard_map/psum | solution.py:137
  597.7 6.1 multiply_reduce_fusion
  604.2 5.5 fusion.42
  612.3 2.2 convolution_convert_fusion.3
  618.5 89.6 %while.25 = (s32[]{:T(128)}, bf16[6,8,64,256]{3,2,1,0:T(8,128)(2,1)}, bf16[6,8,64,256]{3,2,1,0:T(8,128)(2,1)}, bf16[6,8,64,256]{3,2,1,0:T(8,128)(2,1)}, bf16[6,8...) while((s32[]{:T(128)}, ...), condition=%wide.region_17.18_spmd, body=%wide.region_13.17_spmd.sunk | while | flops 86839424 | bytes 17955988 | solution.py:144
  628.5 2.0 convolution_convert_fusion.12
  643.4 2.0 convolution_convert_fusion.12
  658.3 2.0 convolution_convert_fusion.12
  673.2 2.0 convolution_convert_fusion.12
  688.2 2.0 convolution_convert_fusion.12
  708.1 2.6 fusion.48
  710.8 4.2 fusion.49
  716.4 8.2 multiply_reduce_fusion.1
  724.7 5.5 fusion.41
  731.8 6.3 copy.113
  738.1 5.8 all-to-all-start.3
  744.0 9.9 iota_compare_fusion.2
  753.9 15.2 %eq.98 = pred[1536,1024]{1,0:T(32,128)(4,1)} reshape(pred[384,4,32,32]{3,2,1,0:T(32,128)(4,1)} %iota_compare_fusion.2) | data formatting | bytes 3145728 | tf_op jit(solution)/shard_map/eq | solution.py:210
  770.4 5.6 add_convert_fusion
  776.0 5.7 convert_element_type.173
  781.7 8.6 fusion.55
  790.3 7.8 fusion.39
  805.8 9.7 copy.109
  815.5 58.3 %all-to-all-done.3 = f32[48,64,512]{2,0,1:T(8,128)} async-done(((f32[48,64,512]{2,0,1:T(8,128)}), f32[48,64,512]{2,0,1:T(8,128)}, u32[]{:S(2)}, u32[]{:S(2)}) %all-to-all-start.3) | async-done | bytes 6291488 | tf_op jit(solution)/shard_map/all_to_all | solution.py:248
  873.8 9.6 copy.114
  883.4 290.4 %all-reduce.19 = (bf16[768,4,512]{2,1,0:T(4,128)(2,1)}, bf16[768,4,512]{2,1,0:T(4,128)(2,1)}) all-reduce(f32[768,4,512]{2,1,0:T(4,128)} %bitcast.176, f32[768,4,512]{2,1,0:T(4,128)} %bitcast.177), channel_id=2, replica_groups=mesh['gx'=16,'gy'=2] {'gy'}, use_global_device_ids=true, to_apply=%region_9.10.clone | all-reduce | flops 3145728 | bytes 18874368
  1173.7 3.1 dynamic-slice_convert_fusion
  1176.8 2.4 reshape.396
  1179.2 4.6 fusion.50
  1183.8 3.3 convert_reduce_fusion.1
  1187.1 102.3 %all-reduce.3 = (f32[512]{0:T(512)}, f32[512]{0:T(512)}, f32[1024]{0:T(1024)}, f32[512]{0:T(512)}) all-reduce(f32[512]{0:T(512)S(1)} %get-tuple-element.146, f32[512]{0:T(512)S(1)} %get-tuple-element.150, f32[1024]{0:T(1024)S(1)} %copy-done.49, f32[512]{0:T(512)S(1)} %convert_reduce_fusion.1), channel_id=1, replica_groups=mesh['gx'=16,'gy'=2] {'gx'}, use_global_device_ids=true, to_apply=%region_32.33 | all-reduce | flops 2560 | bytes 20480 | tf_op jit(solution)/shard_map/psum | solution.py:288
  1289.9 37.9 %all-reduce.2 = (f32[18,512]{1,0:T(8,128)}, f32[512]{0:T(512)}, f32[512]{0:T(512)}) all-reduce(f32[18,512]{1,0:T(8,128)S(1)} %fusion.33, f32[512]{0:T(512)S(1)} %get-tuple-element.148, f32[512]{0:T(512)S(1)} %get-tuple-element.151), channel_id=1, replica_groups=mesh['gx'=16,'gy'=2] {'gx','gy'}, use_global_device_ids=true, to_apply=%region_22.23 | all-reduce | flops 10240 | bytes 81920 | tf_op jit(solution)/shard_map/psum | solution.py:274
  1327.9 3.1 dynamic-slice_convert_fusion.1
  1331.0 32.4 %all-reduce.16.cloned.1.call-done = f32[1024,512]{1,0:T(8,128)} async-done(((f32[1024,512]{1,0:T(8,128)}), f32[1024,512]{1,0:T(8,128)}) %all-reduce.16.cloned.1.call-update) | async-done | bytes 2097168 | tf_op jit(solution)/shard_map/psum | solution.py:274
  1363.4 3.2 copy.208
  (432 shorter events, 160.5 us)
Async XLA Ops:
  7.2 405.5 %copy-start = (bf16[512,1024]{1,0:T(8,128)(2,1)S(1)}, bf16[512,1024]{1,0:T(8,128)(2,1)}, u32[]{:S(2)}) copy-start(bf16[512,1024]{1,0:T(8,128)(2,1)} %param.36) | copy-start | bytes 3145732
  7.2 86.7 %all-gather.3.cloned.1.call-start = ((), (), s32[]{:S(2)}) async-start(), calls=%async_computation.4 | async-start | bytes 4718592 | tf_op jit(solution)/shard_map/all_gather | solution.py:221
  8.6 9.8 copy-start.17
  18.4 20.0 %copy-start.48 = (s32[384,4]{0,1:T(4,128)S(1)}, s32[384,4]{0,1:T(4,128)}, u32[]{:S(2)}) copy-start(s32[384,4]{0,1:T(4,128)} %param.23) | copy-start | bytes 18436
  38.7 4.9 copy-start.40
  38.7 4.9 copy-start.44
  93.9 65.1 %all-to-all-start = ((bf16[768,4,512]{2,1,0:T(4,128)(2,1)}), bf16[768,4,512]{2,1,0:T(4,128)(2,1)}, u32[]{:S(2)}, u32[]{:S(2)}) async-start(bf16[768,4,512]{2,1,0:T(4,128)(2,1)} %all-gather.3.cloned.1.call-done), calls=%async_computation | async-start | bytes 6291456 | tf_op jit(solution)/shard_map/all_to_all | solution.py:225
  99.5 142.6 %all-gather.5.cloned.1.call-start = ((), (), s32[]{:S(2)}) async-start(), calls=%async_computation.6 | async-start | bytes 4718592 | tf_op jit(solution)/shard_map/all_gather | solution.py:222
  100.3 304.9 %all-reduce.12.cloned.1.call-start = ((), (), s32[]{:S(2)}) async-start(), calls=%async_computation.5 | async-start | bytes 12582912 | tf_op jit(solution)/shard_map/psum | solution.py:120
  162.2 11.0 copy-start.19
  166.9 15.1 %copy-start.34 = (f32[3072]{0:T(1024)}, f32[3072]{0:T(1024)S(1)}, u32[]{:S(2)}) copy-start(f32[3072]{0:T(1024)S(1)} %div.59) | copy-start | bytes 36868
  174.2 7.7 copy-start.38
  174.3 7.7 copy-start.36
  174.3 7.7 copy-start.42
  174.3 7.7 copy-start.45
  182.0 3.8 copy-start.28
  182.0 5.9 copy-start.31
  185.8 4.3 copy-start.32
  193.5 43.5 %copy-start.30 = (bf16[256,512]{1,0:T(8,128)(2,1)S(1)}, bf16[256,512]{1,0:T(8,128)(2,1)}, u32[]{:S(2)}) copy-start(bf16[256,512]{1,0:T(8,128)(2,1)} %param.33) | copy-start | bytes 786436
  242.0 355.7 %all-reduce.14.cloned.1.call-start = ((), (), s32[]{:S(2)}) async-start(), calls=%async_computation.7 | async-start | bytes 12582912 | tf_op jit(solution)/shard_map/psum | solution.py:137
  410.5 12.2 copy-start.3
  412.7 10.0 copy-start.7
  412.7 10.0 copy-start.50
  435.9 2.6 copy-start.57
  461.0 277.1 %all-to-all-start.1 = ((f32[48,64,512]{2,0,1:T(8,128)}), f32[48,64,512]{2,0,1:T(8,128)}, u32[]{:S(2)}, u32[]{:S(2)}) async-start(f32[48,64,512]{2,0,1:T(8,128)} %copy.108), calls=%async_computation.1 | async-start | bytes 12582912 | tf_op jit(solution)/shard_map/all_to_all | solution.py:247
  597.7 6.4 copy-start.10
  604.1 5.5 copy-start.8
  609.6 2.6 copy-start.4
  708.1 2.6 copy-start.12
  708.1 2.7 copy-start.33
  710.7 4.3 slice-start
  710.7 4.3 copy-start.14
  710.7 4.3 copy-start.29
  710.7 4.3 copy-start.35
  710.7 4.3 copy-start.37
  710.7 4.3 copy-start.43
  710.8 5.7 slice-start.1
  710.8 19.4 %slice-start.4 = ((s8[6291456]{0:T(1024)(128)(4,1)}), s8[4194304]{0:T(1024)(128)(4,1)S(1)}, s32[]{:S(2)}) async-start(s8[6291456]{0:T(1024)(128)(4,1)} %bitcast.170), calls=%async_computation.14 | async-start | bytes 8388608
  716.4 8.2 copy-start.39
  716.4 13.8 slice-start.5
  724.6 5.6 copy-start.9
  738.1 5.9 copy-start.18
  738.1 135.6 %all-to-all-start.3 = ((f32[48,64,512]{2,0,1:T(8,128)}), f32[48,64,512]{2,0,1:T(8,128)}, u32[]{:S(2)}, u32[]{:S(2)}) async-start(f32[48,64,512]{2,0,1:T(8,128)} %copy.113), calls=%async_computation.3 | async-start | bytes 12582912 | tf_op jit(solution)/shard_map/all_to_all | solution.py:248
  743.9 587.0 %all-reduce.18.cloned.1.call-start = ((), (), s32[]{:S(2)}) async-start(), calls=%async_computation.9 | async-start | bytes 12582912 | tf_op jit(solution)/shard_map/psum | solution.py:288
  744.0 25.1 %copy-start.55 = (u32[32]{0:T(128)S(1)}, u32[32]{0:T(128)}, u32[]{:S(2)}) copy-start(u32[32]{0:T(128)} %constant.93) | copy-start | bytes 388
  744.0 26.4 %copy-start.20 = (f32[48,16,4]{2,1,0:T(8,128)S(1)}, f32[48,16,4]{2,1,0:T(8,128)}, u32[]{:S(2)}) copy-start(f32[48,16,4]{2,1,0:T(8,128)} %copy-done.19) | copy-start | bytes 36868
  744.0 26.4 %copy-start.25 = (f32[48,16,4]{2,1,0:T(8,128)S(1)}, f32[48,16,4]{2,1,0:T(8,128)}, u32[]{:S(2)}) copy-start(f32[48,16,4]{2,1,0:T(8,128)} %get-tuple-element.209) | copy-start | bytes 36868
  744.0 26.4 %copy-start.46 = (f32[512]{0:T(512)S(1)}, f32[512]{0:T(512)}, u32[]{:S(2)}) copy-start(f32[512]{0:T(512)} %param.29) | copy-start | bytes 6148
  776.0 14.3 %slice-start.2 = ((s8[6291456]{0:T(1024)(128)(4,1)}), s8[2097152]{0:T(1024)(128)(4,1)S(1)}, s32[]{:S(2)}) async-start(s8[6291456]{0:T(1024)(128)(4,1)} %bitcast.168), calls=%async_computation.12 | async-start | bytes 4194304
  781.7 8.6 slice-start.3
  781.7 8.6 copy-start.54
  790.3 7.9 copy-start.16
  790.3 7.9 copy-start.22
  790.3 9.7 copy-start.15
  798.2 3.7 copy-start.13
  800.1 3.6 copy-start.11
  805.5 557.9 %all-reduce.16.cloned.1.call-start = ((), (), s32[]{:S(2)}) async-start(), calls=%async_computation.8 | async-start | bytes 4194304 | tf_op jit(solution)/shard_map/psum | solution.py:274
  1179.2 7.9 copy-start.49
  1179.2 110.2 %copy-start.41 = (s32[1536]{0:T(1024)S(1)}, s32[1536]{0:T(1024)}, u32[]{:S(2)}) copy-start(s32[1536]{0:T(1024)} %copy-done.40) | copy-start | bytes 18436
  1331.0 41.0 %copy-start.24 = (f32[512,1024]{1,0:T(8,128)S(1)}, f32[512,1024]{1,0:T(8,128)}, u32[]{:S(2)}) copy-start(f32[512,1024]{1,0:T(8,128)} %get-tuple-element.383) | copy-start | bytes 6291460
  1363.4 7.0 copy-start.27
  1363.4 7.8 copy-start.26
  1363.4 9.9 copy-start.23
  1363.4 11.2 copy-start.1
  (19 other events, 24.4 us)
Sparse Core Ops, SparseCore 0:
  46.2 47.6 all-gather.2
  101.9 45.2 all-gather.4
  242.1 162.9 all-reduce.11
  444.5 153.1 all-reduce.13
  805.6 207.0 all-reduce.17
  1183.9 179.4 all-reduce.15
where the time goes:
time: 1390 us; the launch traced here: 1380 us
  blocking collectives  516 us (37%)
  waiting for transfers between devices  394 us (28%)
  local copies, waits for them, and re-layouts  220 us (16%)
  matrix products  136 us (10%)
  other arithmetic  80.5 us (6%)
  starting transfers between devices  18.5 us (1%)
  between operations  16 us (1%)
    unnamed x1, blocking collectives  290 us
    psum x1, waiting for transfers between devices, layer_pass(): d_normed_two = lax.psum(d_normed_two, 'gy')  131 us
    psum x1, blocking collectives, per_device(): lax.psum((query_part, key_part, value_part, out_part_grad, second_gain_pa...  102 us
    all_to_all x1, blocking collectives, per_device(): lax.all_to_all(cot_all, 'gx', split_axis=0, concat_axis=1, tiled=True)  85.4 us
    psum x1, waiting for transfers between devices, layer_pass(): branch = lax.psum(branch, 'gy')  67 us
    all_to_all x1, waiting for transfers between devices, per_device(): lax.all_to_all(grad_seq, 'gx', split_axis=1, concat_axis=0, tiled=True)  58.3 us
    all_to_all x1, waiting for transfers between devices, per_device(): lax.all_to_all(token_all, 'gx', split_axis=0, concat_axis=1, tiled=True)  57.1 us
    all_gather x1, waiting for transfers between devices, per_device(): lax.all_gather(tokens, 'gy', axis=0, tiled=True)  47.8 us
  transfers between devices with their start and end apart: 9, of which 6 were waited for; matrix products, arithmetic and copies ran while one was open for 24% of the time, Pallas kernels for 0%

commit v1 on v0

--- a/solution.py
+++ b/solution.py
@@ -1,3 +1,4 @@
+import functools
 import jax
 import jax.numpy as jnp
 from jax import lax
@@ -7,6 +8,23 @@
 EPSILON = 1e-05
 FLOAT = jnp.float32
 BFLOAT = jnp.bfloat16
+
+
+def hubs_shape(sheet, comm_axis):
+    y1, r2 = (lax.axis_size(comm_axis), lax.axis_index(comm_axis))
+    ready = sheet.shape[1] // y1
+    carry_in = jnp.roll(sheet, -r2 * ready, axis=1)
+    table = [lax.slice_in_dim(carry_in, 0, ready, axis=1)]
+    for idx in range(1, y1):
+        value_now = lax.slice_in_dim(carry_in, idx * ready, (idx + 1) * ready, axis=1)
+        table.append(
+            lax.ppermute(value_now, comm_axis, [(jj, (jj + idx) % y1) for jj in range(y1)])
+        )
+    clean = jnp.concatenate(table[::-1], axis=0)
+    return jnp.roll(clean, (r2 + 1) * table[0].shape[0], axis=0)
+
+
+attach_the_stops_all = functools.partial(hubs_shape, comm_axis="gx")
 
 
 def norm_rows(values, gain, bias):
@@ -245,7 +263,7 @@
     out_seq, grad_seq, parts = layer_pass(seq_tokens, seq_cot, seg_rows, weights)
     out_moved, grad_moved = (
         lax.all_to_all(out_seq, "gx", split_axis=1, concat_axis=0, tiled=True),
-        lax.all_to_all(grad_seq, "gx", split_axis=1, concat_axis=0, tiled=True),
+        attach_the_stops_all(grad_seq),
     )
     out_frames, grad_frames = (
         lax.psum_scatter(out_moved, "gy", scatter_dimension=0, tiled=True),

time: 1390 us -> 1440 us (1.036)
  blocking collectives: 516 us -> 466 us
  starting transfers between devices: 18.5 us -> 59 us
  waiting for transfers between devices: 394 us -> 423 us
    ppermute x0 -> x15, waiting for transfers between devices: none -> 145 us  [hubs_shape(): lax.ppermute(value_now, comm_axis, [(jj, (jj + idx) % y1) for jj in range...]
    all_to_all x1 -> x0, waiting for transfers between devices: 58.3 us -> none  [per_device(): lax.all_to_all(grad_seq, 'gx', split_axis=1, concat_axis=0, tiled=True)]
    psum x1, waiting for transfers between devices: 131 us -> 74.8 us  [layer_pass(): d_normed_two = lax.psum(d_normed_two, 'gy')]
    ppermute x0 -> x15, starting transfers between devices: none -> 46.9 us  [hubs_shape(): lax.ppermute(value_now, comm_axis, [(jj, (jj + idx) % y1) for jj in range...]
    psum x1, blocking collectives: 102 us -> 71.6 us  [per_device(): lax.psum((query_part, key_part, value_part, out_part_grad, second_gain_pa...]
    unnamed x1, blocking collectives: 290 us -> 271 us
  transfers between devices with their start and end apart: 9 -> 23, of which waited for: 6 -> 15; matrix products, arithmetic and copies ran while one was open for 24% -> 25% of each run, Pallas kernels for 0% -> 0%
where the time goes in v1:
time: 1440 us
  blocking collectives  466 us (32%)
  waiting for transfers between devices  423 us (29%)
  local copies, waits for them, and re-layouts  232 us (16%)
  matrix products  149 us (10%)
  other arithmetic  90.7 us (6%)
  starting transfers between devices  59 us (4%)
  between operations  15.9 us (1%)
    unnamed x1, blocking collectives  271 us
    ppermute x15, waiting for transfers between devices, hubs_shape(): lax.ppermute(value_now, comm_axis, [(jj, (jj + idx) % y1) for jj in range...  145 us
    all_to_all x1, blocking collectives, per_device(): lax.all_to_all(cot_all, 'gx', split_axis=0, concat_axis=1, tiled=True)  85.4 us
    psum x1, waiting for transfers between devices, layer_pass(): d_normed_two = lax.psum(d_normed_two, 'gy')  74.8 us
    psum x1, blocking collectives, per_device(): lax.psum((query_part, key_part, value_part, out_part_grad, second_gain_pa...  71.6 us
    psum x1, waiting for transfers between devices, layer_pass(): branch = lax.psum(branch, 'gy')  66.8 us
    all_to_all x1, waiting for transfers between devices, per_device(): lax.all_to_all(token_all, 'gx', split_axis=0, concat_axis=1, tiled=True)  56.5 us
    all_gather x1, waiting for transfers between devices, per_device(): lax.all_gather(tokens, 'gy', axis=0, tiled=True)  47.8 us
  transfers between devices with their start and end apart: 23, of which 15 were waited for; matrix products, arithmetic and copies ran while one was open for 25% of the time, Pallas kernels for 0%

profile of v1, /device:TPU:0, one launch (start us, length us, event | category | flops | bytes accessed | tf_op | source)
XLA Modules:
  0.0 1436.3 jit_solution(3040440072022588254)
XLA Ops:
  9.6 9.8 eq.91
  19.4 19.9 %eq.92 = s32[1536,1024]{1,0:T(8,128)} reshape(s32[384,4,32,32]{3,2,1,0:T(8,128)} %eq.91) | data formatting | bytes 12582912 | tf_op jit(solution)/shard_map/eq | solution.py:228
  39.3 4.8 fusion.29
  46.7 47.8 %all-gather.3.cloned.1.call-done = bf16[768,4,512]{2,1,0:T(4,128)(2,1)} async-done(((bf16[384,4,512]{2,1,0:T(4,128)(2,1)}), bf16[768,4,512]{2,1,0:T(4,128)(2,1)}) %all-gather.3.cloned.1.call-update) | async-done | bytes 3145744 | tf_op jit(solution)/shard_map/all_gather | solution.py:239
  94.5 5.7 all-to-all-start
  103.1 56.5 %all-to-all-done = bf16[768,4,512]{2,1,0:T(4,128)(2,1)} async-done(((bf16[768,4,512]{2,1,0:T(4,128)(2,1)}), bf16[768,4,512]{2,1,0:T(4,128)(2,1)}, u32[]{:S(2)}, u32[]{:S(2)}) %all-to-all-start) | async-done | bytes 3145760 | tf_op jit(solution)/shard_map/all_to_all | solution.py:243
  159.6 3.2 fusion.39
  163.0 4.3 multiply_reduce_fusion.5
  167.4 6.3 copy_bitcast_fusion
  174.8 7.6 reshape.397
  182.5 3.8 add_convert_fusion.2
  194.0 58.4 %while.24 = (s32[]{:T(128)}, bf16[6,8,64,256]{3,2,1,0:T(8,128)(2,1)}, bf16[6,8,64,256]{3,2,1,0:T(8,128)(2,1)}, s32[6,8,64]{2,1,0:T(8,128)}, bf16[6,8,64,256]{3,2...) while((s32[]{:T(128)}, bf16[6,8,64,256]{3,2,1,0:T(8,128)(2,1)}, ...), condition=%wide.region_5.6_spmd, body=%wide.region_2.5_spmd.sunk | while | flops 34674816 | bytes 9009281 | solution.py:133
  252.4 5.0 fusion.48
  257.5 85.4 %all_to_all.42 = bf16[768,4,512]{2,1,0:T(4,128)(2,1)S(1)} all-to-all(bf16[768,4,512]{2,1,0:T(4,128)(2,1)} %all-gather.5.cloned.1.call-done), channel_id=1, replica_groups=mesh['gx'=16,'gy'=2] {'gx'}, dimensions={0} | all-to-all | bytes 6291456 | tf_op jit(solution)/shard_map/all_to_all | solution.py:244
  344.6 3.4 copy.142
  348.0 5.8 reshape.390
  353.8 66.8 %all-reduce.12.cloned.1.call-done = f32[3072,512]{1,0:T(8,128)} async-done(((f32[3072,512]{1,0:T(8,128)}), f32[3072,512]{1,0:T(8,128)}) %all-reduce.12.cloned.1.call-update) | async-done | bytes 6291472 | tf_op jit(solution)/shard_map/psum | solution.py:138
  420.6 5.3 fusion.44
  428.2 10.0 multiply_convert_fusion
  438.1 13.3 convert_reduce_fusion
  454.0 5.8 fusion.49
  460.9 9.8 iota_compare_fusion.2
  470.7 15.2 %eq.103 = pred[1536,1024]{1,0:T(32,128)(4,1)} reshape(pred[384,4,32,32]{3,2,1,0:T(32,128)(4,1)} %iota_compare_fusion.2) | data formatting | bytes 3145728 | tf_op jit(solution)/shard_map/eq | solution.py:228
  487.2 5.6 add_convert_fusion
  492.8 5.6 convert_element_type.173
  498.4 10.0 multiply_add_fusion
  508.4 6.3 copy.106
  514.7 5.7 all-to-all-start.1
  520.4 8.5 fusion.57
  528.9 9.5 fusion.40
  538.4 74.8 %all-reduce.14.cloned.1.call-done = f32[3072,512]{1,0:T(8,128)} async-done(((f32[3072,512]{1,0:T(8,128)}), f32[3072,512]{1,0:T(8,128)}) %all-reduce.14.cloned.1.call-update) | async-done | bytes 6291472 | tf_op jit(solution)/shard_map/psum | solution.py:155
  613.2 6.2 multiply_reduce_fusion
  619.6 5.5 fusion.43
  634.0 105.1 %while.25 = (s32[]{:T(128)}, bf16[6,8,64,256]{3,2,1,0:T(8,128)(2,1)}, bf16[6,8,64,256]{3,2,1,0:T(8,128)(2,1)}, bf16[6,8,64,256]{3,2,1,0:T(8,128)(2,1)}, bf16[6,8...) while((s32[]{:T(128)}, ...), condition=%wide.region_17.18_spmd, body=%wide.region_13.17_spmd.sunk | while | flops 86839424 | bytes 17954980 | solution.py:162
  643.1 2.8 convolution_convert_fusion.12
  660.6 2.8 convolution_convert_fusion.12
  678.1 2.8 convolution_convert_fusion.12
  741.7 4.2 fusion.50
  747.4 8.2 multiply_reduce_fusion.1
  755.6 7.8 fusion.42
  763.4 3.8 add_add_fusion.2
  772.1 3.7 collective-permute-start
  787.5 39.0 %collective-permute-done.1 = f32[48,4,512]{2,1,0:T(4,128)S(1)} collective-permute-done((f32[48,4,512]{2,1,0:T(4,128)}, f32[48,4,512]{2,1,0:T(4,128)S(1)}, u32[]{:S(2)}, u32[]{:S(2)}) %collective-permute-start.1) | collective-permute-done | bytes 393248 | tf_op jit(solution)/shard_map/ppermute | solution.py:21
  826.7 5.3 collective-permute-start.7
  832.0 11.3 collective-permute-done.4
  843.4 12.2 collective-permute-done.5
  856.6 8.8 collective-permute-done.6
  865.4 32.0 %collective-permute-start.10 = (f32[48,4,512]{2,1,0:T(4,128)}, f32[48,4,512]{2,1,0:T(4,128)S(1)}, u32[]{:S(2)}, u32[]{:S(2)}) collective-permute-start(f32[48,4,512]{2,1,0:T(4,128)} %get-tuple-element.213), channel_id=1, source_target_pairs={{0,10},{2,12},{4,14},{6,16},{8,18},{10,20},{12,22},{14,24},{16,26}... | collective-permute-start | bytes 1179656 | tf_op jit(solution)/shard_map/ppermute | solution.py:21
  897.5 39.5 %collective-permute-done.7 = f32[48,4,512]{2,1,0:T(4,128)S(1)} collective-permute-done((f32[48,4,512]{2,1,0:T(4,128)}, f32[48,4,512]{2,1,0:T(4,128)S(1)}, u32[]{:S(2)}, u32[]{:S(2)}) %collective-permute-start.7) | collective-permute-done | bytes 393248 | tf_op jit(solution)/shard_map/ppermute | solution.py:21
  937.1 19.7 %collective-permute-done.8 = f32[48,4,512]{2,1,0:T(4,128)S(1)} collective-permute-done((f32[48,4,512]{2,1,0:T(4,128)}, f32[48,4,512]{2,1,0:T(4,128)S(1)}, u32[]{:S(2)}, u32[]{:S(2)}) %collective-permute-start.8) | collective-permute-done | bytes 393248 | tf_op jit(solution)/shard_map/ppermute | solution.py:21
  956.8 3.9 collective-permute-done.9
  962.3 3.7 collective-permute-done.12
  966.0 6.4 collective-permute-done.13
  975.9 3.7 constant_dynamic-slice_fusion.7
  979.6 9.7 copy.107
  989.3 270.8 %all-reduce.19 = (bf16[768,4,512]{2,1,0:T(4,128)(2,1)}, bf16[768,4,512]{2,1,0:T(4,128)(2,1)}) all-reduce(f32[768,4,512]{2,1,0:T(4,128)} %bitcast.170, f32[768,4,512]{2,1,0:T(4,128)} %constant_dynamic-slice_fusion.7), channel_id=2, replica_groups=mesh['gx'=16,'gy'=2] {'gy'}, use_global_device_ids=true, to_apply=%region_9.10.clone | all-reduce | flops 3145728 | bytes 18874368
  1260.2 3.1 dynamic-slice_convert_fusion
  1265.6 4.6 fusion.52
  1270.2 3.3 convert_reduce_fusion.1
  1273.5 71.6 %all-reduce.3 = (f32[512]{0:T(512)}, f32[512]{0:T(512)}, f32[1024]{0:T(1024)}, f32[512]{0:T(512)}) all-reduce(f32[512]{0:T(512)S(1)} %get-tuple-element.146, f32[512]{0:T(512)S(1)} %get-tuple-element.150, f32[1024]{0:T(1024)S(1)} %copy-done.44, f32[512]{0:T(512)S(1)} %convert_reduce_fusion.1), channel_id=1, replica_groups=mesh['gx'=16,'gy'=2] {'gx'}, use_global_device_ids=true, to_apply=%region_32.33 | all-reduce | flops 2560 | bytes 20480 | tf_op jit(solution)/shard_map/psum | solution.py:306
  1345.7 38.0 %all-reduce.2 = (f32[18,512]{1,0:T(8,128)}, f32[512]{0:T(512)}, f32[512]{0:T(512)}) all-reduce(f32[18,512]{1,0:T(8,128)S(1)} %fusion.34, f32[512]{0:T(512)S(1)} %get-tuple-element.148, f32[512]{0:T(512)S(1)} %get-tuple-element.151), channel_id=1, replica_groups=mesh['gx'=16,'gy'=2] {'gx','gy'}, use_global_device_ids=true, to_apply=%region_22.23 | all-reduce | flops 10240 | bytes 81920 | tf_op jit(solution)/shard_map/psum | solution.py:292
  1383.6 3.1 dynamic-slice_convert_fusion.1
  1386.7 31.3 %all-reduce.16.cloned.1.call-done = f32[1024,512]{1,0:T(8,128)} async-done(((f32[1024,512]{1,0:T(8,128)}), f32[1024,512]{1,0:T(8,128)}) %all-reduce.16.cloned.1.call-update) | async-done | bytes 2097168 | tf_op jit(solution)/shard_map/psum | solution.py:292
  1418.1 3.2 copy.234
  (476 shorter events, 225.9 us)
Async XLA Ops:
  7.2 420.9 %copy-start = (bf16[512,1024]{1,0:T(8,128)(2,1)S(1)}, bf16[512,1024]{1,0:T(8,128)(2,1)}, u32[]{:S(2)}) copy-start(bf16[512,1024]{1,0:T(8,128)(2,1)} %param.36) | copy-start | bytes 3145732
  7.2 87.3 %all-gather.3.cloned.1.call-start = ((), (), s32[]{:S(2)}) async-start(), calls=%async_computation.3 | async-start | bytes 4718592 | tf_op jit(solution)/shard_map/all_gather | solution.py:239
  8.4 35.8 %copy-start.38 = (s32[1536]{0:T(1024)}, s32[1536]{0:T(1024)S(1)}, u32[]{:S(2)}) copy-start(s32[1536]{0:T(1024)S(1)} %eq.97) | copy-start | bytes 18436
  9.6 9.8 copy-start.16
  39.3 4.9 copy-start.41
  94.5 65.1 %all-to-all-start = ((bf16[768,4,512]{2,1,0:T(4,128)(2,1)}), bf16[768,4,512]{2,1,0:T(4,128)(2,1)}, u32[]{:S(2)}, u32[]{:S(2)}) async-start(bf16[768,4,512]{2,1,0:T(4,128)(2,1)} %all-gather.3.cloned.1.call-done), calls=%async_computation | async-start | bytes 6291456 | tf_op jit(solution)/shard_map/all_to_all | solution.py:243
  100.2 157.4 %all-gather.5.cloned.1.call-start = ((), (), s32[]{:S(2)}) async-start(), calls=%async_computation.5 | async-start | bytes 4718592 | tf_op jit(solution)/shard_map/all_gather | solution.py:240
  100.9 319.7 %all-reduce.12.cloned.1.call-start = ((), (), s32[]{:S(2)}) async-start(), calls=%async_computation.4 | async-start | bytes 12582912 | tf_op jit(solution)/shard_map/psum | solution.py:138
  163.0 19.4 %copy-start.32 = (f32[3072]{0:T(1024)}, f32[3072]{0:T(1024)S(1)}, u32[]{:S(2)}) copy-start(f32[3072]{0:T(1024)S(1)} %div.59) | copy-start | bytes 36868
  174.7 7.7 copy-start.36
  174.7 7.7 copy-start.34
  174.7 7.7 copy-start.40
  174.8 7.7 copy-start.42
  182.5 5.9 copy-start.30
  257.4 355.7 %all-reduce.14.cloned.1.call-start = ((), (), s32[]{:S(2)}) async-start(), calls=%async_computation.6 | async-start | bytes 12582912 | tf_op jit(solution)/shard_map/psum | solution.py:155
  425.9 12.2 copy-start.3
  428.1 10.0 copy-start.7
  428.1 10.0 copy-start.45
  460.9 25.0 %copy-start.49 = (u32[32]{0:T(128)S(1)}, u32[32]{0:T(128)}, u32[]{:S(2)}) copy-start(u32[32]{0:T(128)} %constant.133) | copy-start | bytes 388
  460.9 26.3 %copy-start.22 = (f32[48,16,4]{2,1,0:T(8,128)S(1)}, f32[48,16,4]{2,1,0:T(8,128)}, u32[]{:S(2)}) copy-start(f32[48,16,4]{2,1,0:T(8,128)} %get-tuple-element.224) | copy-start | bytes 36868
  487.2 11.2 copy-start.47
  514.7 464.9 %all-to-all-start.1 = ((f32[48,64,512]{2,0,1:T(8,128)}), f32[48,64,512]{2,0,1:T(8,128)}, u32[]{:S(2)}, u32[]{:S(2)}) async-start(f32[48,64,512]{2,0,1:T(8,128)} %copy.106), calls=%async_computation.1 | async-start | bytes 12582912 | tf_op jit(solution)/shard_map/all_to_all | solution.py:265
  520.4 866.3 %all-reduce.18.cloned.1.call-start = ((), (), s32[]{:S(2)}) async-start(), calls=%async_computation.8 | async-start | bytes 12582912 | tf_op jit(solution)/shard_map/psum | solution.py:306
  613.2 6.4 copy-start.11
  619.6 5.5 copy-start.8
  634.0 105.1 %copy-start.29 = (bf16[512,256]{1,0:T(8,128)(2,1)S(1)}, bf16[512,256]{1,0:T(8,128)(2,1)}, u32[]{:S(2)}) copy-start(bf16[512,256]{1,0:T(8,128)(2,1)} %param.31) | copy-start | bytes 786436
  741.6 4.3 slice-start
  741.7 4.3 copy-start.14
  741.7 4.3 copy-start.26
  741.7 4.3 copy-start.33
  741.7 4.3 copy-start.35
  741.7 5.7 slice-start.1
  741.7 21.7 %slice-start.2 = ((s8[6291456]{0:T(1024)(128)(4,1)}), s8[4194304]{0:T(1024)(128)(4,1)S(1)}, s32[]{:S(2)}) async-start(s8[6291456]{0:T(1024)(128)(4,1)} %bitcast.164), calls=%async_computation.11 | async-start | bytes 8388608
  747.4 8.2 copy-start.37
  747.4 16.0 %slice-start.3 = ((s8[6291456]{0:T(1024)(128)(4,1)}), s8[2097152]{0:T(1024)(128)(4,1)S(1)}, s32[]{:S(2)}) async-start(s8[6291456]{0:T(1024)(128)(4,1)} %bitcast.164), calls=%async_computation.12 | async-start | bytes 4194304
  755.6 7.8 copy-start.9
  769.4 8.2 copy-start.10
  769.4 6.4 copy-start.5
  772.1 7.4 copy-start.12
  772.1 13.9 collective-permute-start
  777.6 6.2 copy-start.15
  777.6 6.2 copy-start.19
  781.2 45.4 %collective-permute-start.3 = (f32[48,4,512]{2,1,0:T(4,128)}, f32[48,4,512]{2,1,0:T(4,128)S(1)}, u32[]{:S(2)}, u32[]{:S(2)}) collective-permute-start(f32[48,4,512]{2,1,0:T(4,128)} %get-tuple-element.220), channel_id=1, source_target_pairs={{0,24},{2,26},{4,28},{6,30},{8,0},{10,2},{12,4},{14,6},{16,8},{18,... | collective-permute-start | bytes 1179656 | tf_op jit(solution)/shard_map/ppermute | solution.py:21
  782.3 44.2 %collective-permute-start.2 = (f32[48,4,512]{2,1,0:T(4,128)}, f32[48,4,512]{2,1,0:T(4,128)S(1)}, u32[]{:S(2)}, u32[]{:S(2)}) collective-permute-start(f32[48,4,512]{2,1,0:T(4,128)} %get-tuple-element.221), channel_id=1, source_target_pairs={{0,26},{2,28},{4,30},{6,0},{8,2},{10,4},{12,6},{14,8},{16,10},{18,... | collective-permute-start | bytes 1179656 | tf_op jit(solution)/shard_map/ppermute | solution.py:21
  782.3 44.2 %collective-permute-start.1 = (f32[48,4,512]{2,1,0:T(4,128)}, f32[48,4,512]{2,1,0:T(4,128)S(1)}, u32[]{:S(2)}, u32[]{:S(2)}) collective-permute-start(f32[48,4,512]{2,1,0:T(4,128)} %get-tuple-element.222), channel_id=1, source_target_pairs={{0,28},{2,30},{4,0},{6,2},{8,4},{10,6},{12,8},{14,10},{16,12},{18,... | collective-permute-start | bytes 1179656 | tf_op jit(solution)/shard_map/ppermute | solution.py:21
  785.6 186.9 %collective-permute-start.14 = (f32[48,4,512]{2,1,0:T(4,128)S(1)}, f32[48,4,512]{2,1,0:T(4,128)S(1)}, u32[]{:S(2)}, u32[]{:S(2)}) collective-permute-start(f32[48,4,512]{2,1,0:T(4,128)S(1)} %get-tuple-element.209), channel_id=1, source_target_pairs={{0,2},{2,4},{4,6},{6,8},{8,10},{10,12},{12,14},{14,16},{16,18},{18... | collective-permute-start | bytes 1179656 | tf_op jit(solution)/shard_map/ppermute | solution.py:21
  785.9 632.1 %all-reduce.16.cloned.1.call-start = ((), (), s32[]{:S(2)}) async-start(), calls=%async_computation.7 | async-start | bytes 4194304 | tf_op jit(solution)/shard_map/psum | solution.py:292
  786.0 57.3 %collective-permute-start.4 = (f32[48,4,512]{2,1,0:T(4,128)}, f32[48,4,512]{2,1,0:T(4,128)S(1)}, u32[]{:S(2)}, u32[]{:S(2)}) collective-permute-start(f32[48,4,512]{2,1,0:T(4,128)} %get-tuple-element.219), channel_id=1, source_target_pairs={{0,22},{2,24},{4,26},{6,28},{8,30},{10,0},{12,2},{14,4},{16,6},{18... | collective-permute-start | bytes 1179656 | tf_op jit(solution)/shard_map/ppermute | solution.py:21
  826.5 29.1 %collective-permute-start.5 = (f32[48,4,512]{2,1,0:T(4,128)}, f32[48,4,512]{2,1,0:T(4,128)S(1)}, u32[]{:S(2)}, u32[]{:S(2)}) collective-permute-start(f32[48,4,512]{2,1,0:T(4,128)} %get-tuple-element.218), channel_id=1, source_target_pairs={{0,20},{2,22},{4,24},{6,26},{8,28},{10,30},{12,0},{14,2},{16,4},{1... | collective-permute-start | bytes 1179656 | tf_op jit(solution)/shard_map/ppermute | solution.py:21
  826.5 38.9 %collective-permute-start.6 = (f32[48,4,512]{2,1,0:T(4,128)}, f32[48,4,512]{2,1,0:T(4,128)S(1)}, u32[]{:S(2)}, u32[]{:S(2)}) collective-permute-start(f32[48,4,512]{2,1,0:T(4,128)} %get-tuple-element.217), channel_id=1, source_target_pairs={{0,18},{2,20},{4,22},{6,24},{8,26},{10,28},{12,30},{14,0},{16,2},{... | collective-permute-start | bytes 1179656 | tf_op jit(solution)/shard_map/ppermute | solution.py:21
  826.7 110.4 %collective-permute-start.7 = (f32[48,4,512]{2,1,0:T(4,128)}, f32[48,4,512]{2,1,0:T(4,128)S(1)}, u32[]{:S(2)}, u32[]{:S(2)}) collective-permute-start(f32[48,4,512]{2,1,0:T(4,128)} %get-tuple-element.216), channel_id=1, source_target_pairs={{0,16},{2,18},{4,20},{6,22},{8,24},{10,26},{12,28},{14,30},{16,0},... | collective-permute-start | bytes 1179656 | tf_op jit(solution)/shard_map/ppermute | solution.py:21
  843.3 113.5 %collective-permute-start.8 = (f32[48,4,512]{2,1,0:T(4,128)}, f32[48,4,512]{2,1,0:T(4,128)S(1)}, u32[]{:S(2)}, u32[]{:S(2)}) collective-permute-start(f32[48,4,512]{2,1,0:T(4,128)} %get-tuple-element.215), channel_id=1, source_target_pairs={{0,14},{2,16},{4,18},{6,20},{8,22},{10,24},{12,26},{14,28},{16,30}... | collective-permute-start | bytes 1179656 | tf_op jit(solution)/shard_map/ppermute | solution.py:21
  855.5 105.1 %collective-permute-start.9 = (f32[48,4,512]{2,1,0:T(4,128)}, f32[48,4,512]{2,1,0:T(4,128)S(1)}, u32[]{:S(2)}, u32[]{:S(2)}) collective-permute-start(f32[48,4,512]{2,1,0:T(4,128)} %get-tuple-element.214), channel_id=1, source_target_pairs={{0,12},{2,14},{4,16},{6,18},{8,20},{10,22},{12,24},{14,26},{16,28}... | collective-permute-start | bytes 1179656 | tf_op jit(solution)/shard_map/ppermute | solution.py:21
  865.4 96.8 %collective-permute-start.10 = (f32[48,4,512]{2,1,0:T(4,128)}, f32[48,4,512]{2,1,0:T(4,128)S(1)}, u32[]{:S(2)}, u32[]{:S(2)}) collective-permute-start(f32[48,4,512]{2,1,0:T(4,128)} %get-tuple-element.213), channel_id=1, source_target_pairs={{0,10},{2,12},{4,14},{6,16},{8,18},{10,20},{12,22},{14,24},{16,26}... | collective-permute-start | bytes 1179656 | tf_op jit(solution)/shard_map/ppermute | solution.py:21
  937.0 25.2 %collective-permute-start.11 = (f32[48,4,512]{2,1,0:T(4,128)}, f32[48,4,512]{2,1,0:T(4,128)S(1)}, u32[]{:S(2)}, u32[]{:S(2)}) collective-permute-start(f32[48,4,512]{2,1,0:T(4,128)} %get-tuple-element.212), channel_id=1, source_target_pairs={{0,8},{2,10},{4,12},{6,14},{8,16},{10,18},{12,20},{14,22},{16,24},... | collective-permute-start | bytes 1179656 | tf_op jit(solution)/shard_map/ppermute | solution.py:21
  956.8 9.2 collective-permute-start.12
  960.7 11.8 collective-permute-start.13
  1265.6 7.9 copy-start.44
  1265.6 79.5 %copy-start.39 = (s32[1536]{0:T(1024)S(1)}, s32[1536]{0:T(1024)}, u32[]{:S(2)}) copy-start(s32[1536]{0:T(1024)} %copy-done.38) | copy-start | bytes 18436
  1386.7 39.9 %copy-start.21 = (f32[512,1024]{1,0:T(8,128)S(1)}, f32[512,1024]{1,0:T(8,128)}, u32[]{:S(2)}) copy-start(f32[512,1024]{1,0:T(8,128)} %get-tuple-element.398) | copy-start | bytes 6291460
  1418.1 7.0 copy-start.24
  1418.1 7.8 copy-start.23
  1418.1 9.9 copy-start.20
  1418.1 11.2 copy-start.1
  (25 other events, 44.6 us)
Sparse Core Ops, SparseCore 0:
  46.8 47.6 all-gather.2
  102.5 45.2 all-gather.4
  257.6 162.9 all-reduce.11
  460.0 153.1 all-reduce.13
  786.1 245.6 all-reduce.17
  1270.3 147.6 all-reduce.15
